TPU v7x, 512 devices: a whole 4x8x8 slice. The times are simulated.
512 devices in a mesh: ctx: 8 (over x, core), dp: 8 (over y), mp: 8 (over z).
Axes of the slice: x: 4, y: 8, z: 8, core: 2. Of those that a mesh axis runs over, the one named last changes fastest.
Arguments:
- queries: bfloat16 [16384, 5120], P(('ctx', 'dp'), 'mp'), may hold values from -200 to 200, as said below
- suffix_keys: bfloat16 [16384, 1024], P(('ctx', 'dp'), 'mp'), may hold values from -6 to 6
- suffix_values: bfloat16 [16384, 1024], P(('ctx', 'dp'), 'mp'), may hold values from -6 to 6
- pre_keys: bfloat16 [3072, 1024], P('ctx', 'mp'), may hold values from -6 to 6
- pre_values: bfloat16 [3072, 1024], P('ctx', 'mp'), may hold values from -6 to 6
- segments: int32 [64, 256], P(('ctx', 'dp')), may hold values from 0 to 7, never falling along the last dimension, each value on 1 to 64 neighbouring positions
- d_out: bfloat16 [16384, 5120], P(('ctx', 'dp'), 'mp'), may hold values from -6 to 6
Outputs:
- attended: bfloat16 [16384, 5120], P(('ctx', 'dp'), 'mp')
- d_queries: bfloat16 [16384, 5120], P(('ctx', 'dp'), 'mp')
- suffix_keys_gradient: bfloat16 [16384, 1024], P(('ctx', 'dp'), 'mp')
- suffix_values_gradient: bfloat16 [16384, 1024], P(('ctx', 'dp'), 'mp')
- d_pre_keys: float32 [3072, 1024], P(('ctx', 'dp'), 'mp')
- d_pre_values: float32 [3072, 1024], P(('ctx', 'dp'), 'mp')
Inputs may be any that keep to these rules, and one draw needn't show every extreme that they name: `queries`: scaled Gaussian entries.
All inputs are finite; a program needn't handle non-finite values.
Results may differ from a plain program's by a relative error of at most 0.023.
Values may be sent and summed in bfloat16 or wider, within the bound.
A program may use at most 64 MiB of HBM per device.

v0:
```python
import jax
import jax.numpy as jnp
from jax import lax
from jax.sharding import PartitionSpec as P

HEAD_WIDTH = 128
Q_HEADS = 40
KEY_VALUE_HEADS = 8


def contract_rows(left, right):
    return lax.dot_general(
        left, right, (((0,), (0,)), ((), ())), preferred_element_type=jnp.float32
    )


def contract_cols(left, right):
    return lax.dot_general(
        left, right, (((1,), (1,)), ((), ())), preferred_element_type=jnp.float32
    )


def stack_heads(matrix, count):
    rows = matrix.shape[0]
    return matrix.reshape(rows, count, HEAD_WIDTH).transpose(1, 0, 2)


def unstack_heads(stacked):
    count, rows, width = stacked.shape
    return stacked.transpose(1, 0, 2).reshape(rows, count * width)


def shards(queries, suffix_keys, suffix_values, pre_keys, pre_values, segments, d_out):
    per_group = Q_HEADS // KEY_VALUE_HEADS
    att_scale = HEAD_WIDTH ** (-0.5)
    all_keys, all_values = (
        lax.all_gather(pre_keys, "ctx", axis=0, tiled=True),
        lax.all_gather(pre_values, "ctx", axis=0, tiled=True),
    )
    prefix_len = all_keys.shape[0]
    tok_count = queries.shape[0]
    kv_local = suffix_keys.shape[1] // HEAD_WIDTH
    segment_index = segments[0]
    row_ids = lax.broadcasted_iota(jnp.int32, (tok_count, tok_count), 0)
    col_ids = lax.broadcasted_iota(jnp.int32, (tok_count, tok_count), 1)
    local_ok = (segment_index[:, None] == segment_index[None, :]) & (col_ids <= row_ids)
    allowed = jnp.concatenate([jnp.ones((tok_count, prefix_len), bool), local_ok], 1)
    out_list, dq_list, dk_list, dv_list = ([], [], [], [])
    top_list, total_list, delta_list = ([], [], [])
    joined_keys = jnp.concatenate([all_keys, suffix_keys], 0)
    joined_values = jnp.concatenate([all_values, suffix_values], 0)
    grad_rows = prefix_len + tok_count

    def head_step(carry, head_entries):
        key_grad, value_grad = carry
        query_rows, output_gradient = head_entries
        scores = contract_cols(query_rows, joined_keys) * att_scale
        scores = jnp.where(allowed, scores, -1e30)
        top = jnp.max(scores, -1, keepdims=True)
        expo = jnp.exp(scores - top)
        total = jnp.sum(expo, -1, keepdims=True)
        weights = expo / total
        weights_bf = weights.astype(jnp.bfloat16)
        out = jnp.dot(weights_bf, joined_values, preferred_element_type=jnp.float32)
        delta = jnp.sum(output_gradient.astype(jnp.float32) * out, -1, keepdims=True)
        d_weights = contract_cols(output_gradient, joined_values)
        d_scores = (weights * (d_weights - delta)).astype(jnp.bfloat16)
        query_gradient = (
            jnp.dot(d_scores, joined_keys, preferred_element_type=jnp.float32) * att_scale
        )
        key_grad = key_grad + contract_rows(d_scores, query_rows) * att_scale
        value_grad = value_grad + contract_rows(weights_bf, output_gradient)
        return (
            (key_grad, value_grad),
            (out.astype(jnp.bfloat16), query_gradient.astype(jnp.bfloat16), top, total, delta),
        )

    start_grads = (
        jnp.zeros((grad_rows, HEAD_WIDTH), jnp.float32),
        jnp.zeros((grad_rows, HEAD_WIDTH), jnp.float32),
    )
    head_inputs = (stack_heads(queries, per_group), stack_heads(d_out, per_group))
    (key_grad, value_grad), (outs_st, dqs_st, tops_st, totals_st, deltas_st) = lax.scan(
        head_step, start_grads, head_inputs
    )
    out_list.append(unstack_heads(outs_st))
    dq_list.append(unstack_heads(dqs_st))
    top_list.append(unstack_heads(tops_st))
    total_list.append(unstack_heads(totals_st))
    delta_list.append(unstack_heads(deltas_st))
    dk_list.append(key_grad)
    dv_list.append(value_grad)
    attended = out_list[0]
    d_queries = dq_list[0]
    key_grads = dk_list[0]
    value_grads = dv_list[0]
    width = kv_local * HEAD_WIDTH
    suffix_keys_gradient = key_grads[prefix_len:].astype(jnp.bfloat16)
    suffix_values_gradient = value_grads[prefix_len:].astype(jnp.bfloat16)
    prefix_terms = jnp.concatenate([key_grads[:prefix_len], value_grads[:prefix_len]], 1)
    share = lax.psum_scatter(prefix_terms, ("ctx", "dp"), scatter_dimension=0, tiled=True)
    return (
        attended,
        d_queries,
        suffix_keys_gradient,
        suffix_values_gradient,
        share[:, :width],
        share[:, width:],
    )


def solution(mesh):
    in_specs = (
        P(("ctx", "dp"), "mp"),
        P(("ctx", "dp"), "mp"),
        P(("ctx", "dp"), "mp"),
        P("ctx", "mp"),
        P("ctx", "mp"),
        P(("ctx", "dp"), None),
        P(("ctx", "dp"), "mp"),
    )
    out_specs = (
        P(("ctx", "dp"), "mp"),
        P(("ctx", "dp"), "mp"),
        P(("ctx", "dp"), "mp"),
        P(("ctx", "dp"), "mp"),
        P(("ctx", "dp"), "mp"),
        P(("ctx", "dp"), "mp"),
    )
    return jax.shard_map(shards, mesh=mesh, in_specs=in_specs, out_specs=out_specs, check_vma=False)
```

profile of v0, /device:TPU:6, one launch (start us, length us, event | category | flops | bytes accessed | tf_op | source)
XLA Modules:
  0.0 297.6 jit_solution(8986499974697198335)
XLA Ops:
  9.6 16.8 %all_gather.6 = bf16[3072,128]{1,0:T(8,128)(2,1)S(1)} all-gather(bf16[384,128]{1,0:T(8,128)(2,1)S(1)} %copy-done.9), channel_id=1, replica_groups=mesh['ctx'=8,'dp'=8,'mp'=8] {'ctx'}, dimensions={0}, use_global_device_ids=true | all-gather | bytes 884736 | tf_op jit(solution)/shard_map/all_gather | solution.py:37
  26.4 13.4 %all_gather.7 = bf16[3072,128]{1,0:T(8,128)(2,1)S(1)} all-gather(bf16[384,128]{1,0:T(8,128)(2,1)S(1)} %copy-done.10), channel_id=1, replica_groups=mesh['ctx'=8,'dp'=8,'mp'=8] {'ctx'}, dimensions={0}, use_global_device_ids=true | all-gather | bytes 884736 | tf_op jit(solution)/shard_map/all_gather | solution.py:38
  43.5 91.3 %while.17 = (s32[]{:T(128)}, f32[3328,128]{1,0:T(8,128)}, f32[3328,128]{1,0:T(8,128)}, bf16[5,256,128]{1,2,0:T(8,128)(2,1)}, bf16[5,256,128]{1,2,0:T(8,128)(2,1)...) while((s32[]{:T(128)}, f32[3328,128]{1,0:T(8,128)}, ...), condition=%wide.region_4.5_spmd.clone, body=%wide.region_0.4_spmd.clone.sunk | while | flops 1324580096 | bytes 54540016 | solution.py:83
  43.5 2.3 fusion.59
  47.0 2.4 multiply_reduce_fusion.2
  49.4 2.0 fusion.61
  54.8 3.1 %convolution_add_fusion.2 = f32[3328,128]{1,0:T(8,128)} fusion(f32[3328,128]{1,0:T(8,128)} %get-tuple-element.241, pred[]{:T(512)S(6)} %compare.4, bf16[5,256,128]{1,2,0:T(8,128)(2,1)} %get-tuple-element.259, s32[]{:T(128)} %get-tuple-element.239, f32[256,3328]{1,0:T(8,128)S(1)} %get-tuple-element.221, f32[256]{0:T(256)S(1)} %fusion.60, ...), kind=kOutput, calls=%fused_computation.5.clone.1 | convolution fusion | flops 221511680 | bytes 6883841 | tf_op jit(solution)/shard_map/while/body/eval_jaxpr/dot_general | solution.py:12
  58.0 2.7 fusion.62
  60.7 2.3 fusion.59
  64.2 2.4 multiply_reduce_fusion.2
  66.6 2.0 fusion.61
  72.1 3.8 %convolution_add_fusion.2 = f32[3328,128]{1,0:T(8,128)} fusion(f32[3328,128]{1,0:T(8,128)} %get-tuple-element.241, pred[]{:T(512)S(6)} %compare.4, bf16[5,256,128]{1,2,0:T(8,128)(2,1)} %get-tuple-element.259, s32[]{:T(128)} %get-tuple-element.239, f32[256,3328]{1,0:T(8,128)S(1)} %get-tuple-element.221, f32[256]{0:T(256)S(1)} %fusion.60, ...), kind=kOutput, calls=%fused_computation.5.clone.1 | convolution fusion | flops 221511680 | bytes 6883841 | tf_op jit(solution)/shard_map/while/body/eval_jaxpr/dot_general | solution.py:12
  75.8 3.4 %fusion.62 = f32[3328,128]{1,0:T(8,128)} fusion(bf16[256,3328]{1,0:T(8,128)(2,1)S(1)} %copy-done.1, f32[3328,128]{1,0:T(8,128)} %get-tuple-element.240, pred[]{:T(512)S(6)} %compare.4, bf16[5,256,128]{1,2,0:T(8,128)(2,1)} %get-tuple-element.256, s32[]{:T(128)} %get-tuple-element.239), kind=kOutput, calls=%fused_computation.7.clone.1 | convolution fusion | flops 219381760 | bytes 5177857 | tf_op jit(solution)/shard_map/while/body/eval_jaxpr/dot_general | solution.py:12
  79.2 2.3 fusion.59
  82.7 2.4 multiply_reduce_fusion.2
  85.1 2.0 fusion.61
  90.6 3.8 %convolution_add_fusion.2 = f32[3328,128]{1,0:T(8,128)} fusion(f32[3328,128]{1,0:T(8,128)} %get-tuple-element.241, pred[]{:T(512)S(6)} %compare.4, bf16[5,256,128]{1,2,0:T(8,128)(2,1)} %get-tuple-element.259, s32[]{:T(128)} %get-tuple-element.239, f32[256,3328]{1,0:T(8,128)S(1)} %get-tuple-element.221, f32[256]{0:T(256)S(1)} %fusion.60, ...), kind=kOutput, calls=%fused_computation.5.clone.1 | convolution fusion | flops 221511680 | bytes 6883841 | tf_op jit(solution)/shard_map/while/body/eval_jaxpr/dot_general | solution.py:12
  94.3 3.4 %fusion.62 = f32[3328,128]{1,0:T(8,128)} fusion(bf16[256,3328]{1,0:T(8,128)(2,1)S(1)} %copy-done.1, f32[3328,128]{1,0:T(8,128)} %get-tuple-element.240, pred[]{:T(512)S(6)} %compare.4, bf16[5,256,128]{1,2,0:T(8,128)(2,1)} %get-tuple-element.256, s32[]{:T(128)} %get-tuple-element.239), kind=kOutput, calls=%fused_computation.7.clone.1 | convolution fusion | flops 219381760 | bytes 5177857 | tf_op jit(solution)/shard_map/while/body/eval_jaxpr/dot_general | solution.py:12
  97.7 2.3 fusion.59
  101.2 2.4 multiply_reduce_fusion.2
  103.6 2.0 fusion.61
  109.1 3.8 %convolution_add_fusion.2 = f32[3328,128]{1,0:T(8,128)} fusion(f32[3328,128]{1,0:T(8,128)} %get-tuple-element.241, pred[]{:T(512)S(6)} %compare.4, bf16[5,256,128]{1,2,0:T(8,128)(2,1)} %get-tuple-element.259, s32[]{:T(128)} %get-tuple-element.239, f32[256,3328]{1,0:T(8,128)S(1)} %get-tuple-element.221, f32[256]{0:T(256)S(1)} %fusion.60, ...), kind=kOutput, calls=%fused_computation.5.clone.1 | convolution fusion | flops 221511680 | bytes 6883841 | tf_op jit(solution)/shard_map/while/body/eval_jaxpr/dot_general | solution.py:12
  112.9 3.4 %fusion.62 = f32[3328,128]{1,0:T(8,128)} fusion(bf16[256,3328]{1,0:T(8,128)(2,1)S(1)} %copy-done.1, f32[3328,128]{1,0:T(8,128)} %get-tuple-element.240, pred[]{:T(512)S(6)} %compare.4, bf16[5,256,128]{1,2,0:T(8,128)(2,1)} %get-tuple-element.256, s32[]{:T(128)} %get-tuple-element.239), kind=kOutput, calls=%fused_computation.7.clone.1 | convolution fusion | flops 219381760 | bytes 5177857 | tf_op jit(solution)/shard_map/while/body/eval_jaxpr/dot_general | solution.py:12
  116.3 2.3 fusion.59
  119.8 2.4 multiply_reduce_fusion.2
  122.1 2.0 fusion.61
  127.6 3.8 %convolution_add_fusion.2 = f32[3328,128]{1,0:T(8,128)} fusion(f32[3328,128]{1,0:T(8,128)} %get-tuple-element.241, pred[]{:T(512)S(6)} %compare.4, bf16[5,256,128]{1,2,0:T(8,128)(2,1)} %get-tuple-element.259, s32[]{:T(128)} %get-tuple-element.239, f32[256,3328]{1,0:T(8,128)S(1)} %get-tuple-element.221, f32[256]{0:T(256)S(1)} %fusion.60, ...), kind=kOutput, calls=%fused_computation.5.clone.1 | convolution fusion | flops 221511680 | bytes 6883841 | tf_op jit(solution)/shard_map/while/body/eval_jaxpr/dot_general | solution.py:12
  131.4 3.4 %fusion.62 = f32[3328,128]{1,0:T(8,128)} fusion(bf16[256,3328]{1,0:T(8,128)(2,1)S(1)} %copy-done.1, f32[3328,128]{1,0:T(8,128)} %get-tuple-element.240, pred[]{:T(512)S(6)} %compare.4, bf16[5,256,128]{1,2,0:T(8,128)(2,1)} %get-tuple-element.256, s32[]{:T(128)} %get-tuple-element.239), kind=kOutput, calls=%fused_computation.7.clone.1 | convolution fusion | flops 219381760 | bytes 5177857 | tf_op jit(solution)/shard_map/while/body/eval_jaxpr/dot_general | solution.py:12
  134.8 1.6 slice.22
  136.8 1.9 pad_maximum_fusion
  139.3 1.5 slice.33
  142.7 146.7 %reduce-scatter.2.cloned.1.call-done = f32[48,256]{1,0:T(8,128)} async-done(((f32[3072,256]{1,0:T(8,128)}), f32[48,256]{1,0:T(8,128)}) %reduce-scatter.2.cloned.1.call-update) | async-done | bytes 49168 | tf_op jit(solution)/shard_map/reduce_scatter | solution.py:101
  (96 shorter events, 33.1 us)
Async XLA Ops:
  7.2 2.4 copy-start.9
  7.2 282.2 %reduce-scatter.2.cloned.1.call-start = ((), (), s32[]{:S(2)}) async-start(), calls=%async_computation.1 | async-start | bytes 3194880 | tf_op jit(solution)/shard_map/reduce_scatter | solution.py:101
  8.1 18.3 %copy-start.10 = (bf16[384,128]{1,0:T(8,128)(2,1)S(1)}, bf16[384,128]{1,0:T(8,128)(2,1)}, u32[]{:S(2)}) copy-start(bf16[384,128]{1,0:T(8,128)(2,1)} %param.13) | copy-start | bytes 294916
  8.4 31.4 %copy-start.5 = (bf16[256,640]{1,0:T(8,128)(2,1)S(1)}, bf16[256,640]{1,0:T(8,128)(2,1)}, u32[]{:S(2)}) copy-start(bf16[256,640]{1,0:T(8,128)(2,1)} %param.9) | copy-start | bytes 983044
  8.4 32.3 %copy-start.6 = (bf16[256,640]{1,0:T(8,128)(2,1)S(1)}, bf16[256,640]{1,0:T(8,128)(2,1)}, u32[]{:S(2)}) copy-start(bf16[256,640]{1,0:T(8,128)(2,1)} %param.15) | copy-start | bytes 983044
  9.6 32.0 %copy-start.11 = (bf16[256,128]{1,0:T(8,128)(2,1)S(1)}, bf16[256,128]{1,0:T(8,128)(2,1)}, u32[]{:S(2)}) copy-start(bf16[256,128]{1,0:T(8,128)(2,1)} %param.10) | copy-start | bytes 196612
  39.8 2.8 copy-start.12
  45.8 1.2 copy-start.4
  49.4 3.3 %copy-start.2 = (bf16[3328,128]{1,0:T(8,128)(2,1)S(1)}, bf16[3328,128]{1,0:T(8,128)(2,1)}, u32[]{:S(2)}) copy-start(bf16[3328,128]{1,0:T(8,128)(2,1)} %get-tuple-element.257) | copy-start | bytes 2555908 | tf_op jit(solution)/shard_map/while
  51.4 1.2 copy-start
  54.8 3.1 %copy-start.1 = (bf16[256,3328]{1,0:T(8,128)(2,1)S(1)}, bf16[256,3328]{1,0:T(8,128)(2,1)}, u32[]{:S(2)}) copy-start(bf16[256,3328]{1,0:T(8,128)(2,1)} %copy-done) | copy-start | bytes 5111812 | tf_op jit(solution)/shard_map/while
  63.0 1.2 copy-start.4
  66.6 3.3 %copy-start.2 = (bf16[3328,128]{1,0:T(8,128)(2,1)S(1)}, bf16[3328,128]{1,0:T(8,128)(2,1)}, u32[]{:S(2)}) copy-start(bf16[3328,128]{1,0:T(8,128)(2,1)} %get-tuple-element.257) | copy-start | bytes 2555908 | tf_op jit(solution)/shard_map/while
  68.6 1.2 copy-start
  72.1 3.8 %copy-start.1 = (bf16[256,3328]{1,0:T(8,128)(2,1)S(1)}, bf16[256,3328]{1,0:T(8,128)(2,1)}, u32[]{:S(2)}) copy-start(bf16[256,3328]{1,0:T(8,128)(2,1)} %copy-done) | copy-start | bytes 5111812 | tf_op jit(solution)/shard_map/while
  81.6 1.2 copy-start.4
  85.1 3.3 %copy-start.2 = (bf16[3328,128]{1,0:T(8,128)(2,1)S(1)}, bf16[3328,128]{1,0:T(8,128)(2,1)}, u32[]{:S(2)}) copy-start(bf16[3328,128]{1,0:T(8,128)(2,1)} %get-tuple-element.257) | copy-start | bytes 2555908 | tf_op jit(solution)/shard_map/while
  87.2 1.2 copy-start
  90.6 3.8 %copy-start.1 = (bf16[256,3328]{1,0:T(8,128)(2,1)S(1)}, bf16[256,3328]{1,0:T(8,128)(2,1)}, u32[]{:S(2)}) copy-start(bf16[256,3328]{1,0:T(8,128)(2,1)} %copy-done) | copy-start | bytes 5111812 | tf_op jit(solution)/shard_map/while
  100.1 1.2 copy-start.4
  103.6 3.3 %copy-start.2 = (bf16[3328,128]{1,0:T(8,128)(2,1)S(1)}, bf16[3328,128]{1,0:T(8,128)(2,1)}, u32[]{:S(2)}) copy-start(bf16[3328,128]{1,0:T(8,128)(2,1)} %get-tuple-element.257) | copy-start | bytes 2555908 | tf_op jit(solution)/shard_map/while
  105.7 1.2 copy-start
  109.1 3.8 %copy-start.1 = (bf16[256,3328]{1,0:T(8,128)(2,1)S(1)}, bf16[256,3328]{1,0:T(8,128)(2,1)}, u32[]{:S(2)}) copy-start(bf16[256,3328]{1,0:T(8,128)(2,1)} %copy-done) | copy-start | bytes 5111812 | tf_op jit(solution)/shard_map/while
  118.6 1.2 copy-start.4
  122.1 3.3 %copy-start.2 = (bf16[3328,128]{1,0:T(8,128)(2,1)S(1)}, bf16[3328,128]{1,0:T(8,128)(2,1)}, u32[]{:S(2)}) copy-start(bf16[3328,128]{1,0:T(8,128)(2,1)} %get-tuple-element.257) | copy-start | bytes 2555908 | tf_op jit(solution)/shard_map/while
  124.2 1.2 copy-start
  127.6 3.8 %copy-start.1 = (bf16[256,3328]{1,0:T(8,128)(2,1)S(1)}, bf16[256,3328]{1,0:T(8,128)(2,1)}, u32[]{:S(2)}) copy-start(bf16[256,3328]{1,0:T(8,128)(2,1)} %copy-done) | copy-start | bytes 5111812 | tf_op jit(solution)/shard_map/while
  134.8 1.9 copy-start.3
  138.7 2.2 copy-start.7
  138.7 3.1 %copy-start.8 = (bf16[5,256,128]{1,2,0:T(8,128)(2,1)S(1)}, bf16[5,256,128]{1,2,0:T(8,128)(2,1)}, u32[]{:S(2)}) copy-start(bf16[5,256,128]{1,2,0:T(8,128)(2,1)} %get-tuple-element.62) | copy-start | bytes 983044
Sparse Core Ops, SparseCore 0:
  138.8 150.5 reduce-scatter.1
where the time goes:
time: 300 us; the launch traced here: 298 us
  waiting for transfers between devices  147 us (49%)
  matrix products  71.3 us (24%)
  blocking collectives  30.2 us (10%)
  local copies, waits for them, and re-layouts  27.4 us (9%)
  between operations  14.1 us (5%)
  other arithmetic  7.68 us (3%)
    reduce_scatter x1, waiting for transfers between devices, shards(): lax.psum_scatter(prefix_terms, ('ctx', 'dp'), scatter_dimension=0, tiled=...  147 us
    dot_general x10, matrix products, contract_rows(): lax.dot_general(left, right, (((0,), (0,)), ((), ())), preferred_element_...  34.5 us
    dot_general x10, matrix products, contract_cols(): lax.dot_general(left, right, (((1,), (1,)), ((), ())), preferred_element_...  21.8 us
    all_gather x1, blocking collectives, shards(): lax.all_gather(pre_keys, 'ctx', axis=0, tiled=True)  16.8 us
    all_gather x1, blocking collectives, shards(): lax.all_gather(pre_values, 'ctx', axis=0, tiled=True)  13.4 us
    dot_general x5, matrix products, head_step(): out = jnp.dot(weights_bf, joined_values, preferred_element_type=jnp.float32)  11.9 us
    while x40, local copies, waits for them, and re-layouts  8.76 us
    dynamic_update_slice x10, local copies, waits for them, and re-layouts, shards(): lax.scan(head_step, start_grads, head_inputs)  7.99 us
  transfers between devices with their start and end apart: 1, of which 1 were waited for; matrix products, arithmetic and copies ran while one was open for 1% of the time, Pallas kernels for 0%

commit v1 on v0

v1 whole, which is shorter than its diff:
```python
import jax
import jax.numpy as jnp
from jax import lax
from jax.experimental import pallas as pl
from jax.experimental.pallas import tpu as pltpu
from jax.sharding import PartitionSpec as P

HEAD_WIDTH = 128
HEADS = 5
TOKENS = 256
ROWS = HEADS * TOKENS
OWN = 384
PIECE = 48
SCALE = HEAD_WIDTH ** (-0.5)
LOG2_SCALE = 1.4426950408889634 * SCALE
MESH = pl.DeviceIdType.MESH
bf16 = jnp.bfloat16
f32 = jnp.float32

KEYS = TOKENS + 8 * OWN
SLOT = [TOKENS + OWN * i for i in range(8)]
CHUNKS = [(0, 640), (640, 384), (1024, 768), (1792, 768), (2560, 384), (2944, 384)]
CHUNK_OF_SLOT = [0, 1, 2, 2, 3, 3, 4, 5]
STRIP = 256


def dot(left, right):
    return lax.dot_general(left, right, (((1,), (0,)), ((), ())), preferred_element_type=f32)


def head_cols(head):
    return slice(head * TOKENS, (head + 1) * TOKENS)


def strips(count):
    return [(at, min(STRIP, count - at)) for at in range(0, count, STRIP)]


def kernel(
    q_ref, sk_ref, sv_ref, pk_ref, pv_ref, seg_ref, do_ref,
    out_ref, dq_ref, dsk_ref, dsv_ref, dpk_ref, dpv_ref,
    kv, qT, dT, qs, ds, kT, vT, k2, bias, top, total, acc, tops, delta, factor, s_buf, p_buf, d_buf,
    keep, sib_send, sib_recv, x_send, x_recv, y_send, y_recv,
    ag_s, ag_r, sib_s, sib_r, x_s, x_r, y_s, y_r,
):
    ctx = lax.axis_index("ctx")
    dp = lax.axis_index("dp")
    core = ctx % 2
    chip = ctx // 2
    ahead = ((chip + 1 + 2 * core) % 4) * 2 + core
    behind = ((chip + 3 + 2 * core) % 4) * 2 + core
    other = chip * 2 + (1 - core)

    barrier = pltpu.get_barrier_semaphore()
    for peer in (ahead, behind, other):
        pl.semaphore_signal(barrier, inc=1, device_id={"ctx": peer}, device_id_type=MESH)
    for step in range(1, 8):
        pl.semaphore_signal(barrier, inc=1, device_id={"dp": (dp + step) % 8}, device_id_type=MESH)

    def send(src, dst, s_sem, r_sem, device):
        copy = pltpu.make_async_remote_copy(
            src_ref=src, dst_ref=dst, send_sem=s_sem, recv_sem=r_sem, device_id=device, device_id_type=MESH
        )
        copy.start()
        return copy

    def spread(index, source, slot, peer):
        return send(kv.at[source], kv.at[slot], ag_s.at[index], ag_r.at[slot], {"ctx": peer})

    def arrived(slot):
        pltpu.make_async_remote_copy(
            src_ref=kv.at[slot], dst_ref=kv.at[slot], send_sem=ag_s.at[0], recv_sem=ag_r.at[slot],
            device_id={"ctx": other}, device_id_type=MESH,
        ).wait_recv()

    def prepare_keys(start, keys, values):
        count = keys.shape[0]
        kT[:, start:start + count] = keys.T
        vT[0:128, start:start + count] = values.T
        scaled = keys.astype(f32) * LOG2_SCALE
        high = scaled.astype(bf16)
        k2[start:start + count, 0:128] = high
        k2[start:start + count, 128:256] = (scaled - high.astype(f32)).astype(bf16)

    kv[0, 0] = pk_ref[...]
    kv[0, 1] = pv_ref[...]
    pl.semaphore_wait(barrier, 10)
    sends = [spread(0, 0, 3, ahead), spread(1, 0, 2, behind), spread(2, 0, 1, other)]

    for head in range(HEADS):
        cols = head_cols(head)
        width = slice(head * 128, (head + 1) * 128)
        q_head, do_head = q_ref[:, width], do_ref[:, width]
        q_turned = q_head.T
        qT[0:128, cols] = q_turned
        qT[128:256, cols] = q_turned
        dT[:, cols] = do_head.T
        qs[cols, :] = q_head
        ds[cols, :] = do_head
    seg = jnp.broadcast_to(seg_ref[...].astype(f32), (TOKENS, TOKENS))
    key_id = lax.broadcasted_iota(jnp.int32, (TOKENS, TOKENS), 0)
    token_id = lax.broadcasted_iota(jnp.int32, (TOKENS, TOKENS), 1)
    bias[...] = jnp.where((seg == seg.T) & (key_id <= token_id), 0.0, -1e30)
    vT[128:144, :] = jnp.where(lax.broadcasted_iota(jnp.int32, (16, KEYS), 0) == 0, 1.0, 0.0).astype(bf16)
    prepare_keys(0, sk_ref[...], sv_ref[...])
    prepare_keys(SLOT[0], pk_ref[...], pv_ref[...])

    def ready(slot):
        prepare_keys(SLOT[slot], kv[slot, 0], kv[slot, 1])

    def before_chunk(chunk):
        if chunk == 1:
            arrived(1)
            ready(1)
        if chunk == 2:
            arrived(3)
            sends.append(spread(3, 3, 6, ahead))
            sends.append(spread(4, 3, 4, other))
            arrived(2)
            sends.append(spread(5, 2, 5, other))
            ready(2)
            ready(3)
        if chunk == 3:
            arrived(4)
            arrived(5)
            ready(4)
            ready(5)
        if chunk == 4:
            arrived(6)
            sends.append(spread(6, 6, 7, other))
            ready(6)
        if chunk == 5:
            arrived(7)
            ready(7)

    steps = [(chunk, head) for chunk in range(len(CHUNKS)) for head in range(HEADS)]
    peak, fade = {}, {}

    def score_strip(index, at, count):
        chunk, head = steps[index]
        start = CHUNKS[chunk][0] + at
        s = dot(k2[start:start + count, :], qT[:, head_cols(head)])
        if chunk == 0 and at < TOKENS:
            s = s + bias[at:at + count, :]
        s_buf[index % 2, at:at + count, :] = s
        part = jnp.max(s.reshape(count // 8, 8, TOKENS), 0)
        peak[index] = part if index not in peak else jnp.maximum(peak[index], part)

    def finish_peak(index):
        chunk, head = steps[index]
        cols = head_cols(head)
        highest = jnp.max(peak[index], 0, keepdims=True)
        if chunk > 0:
            before = top[:, cols]
            highest = jnp.maximum(highest, before)
            fade[index] = jnp.exp2(before - highest)
        top[:, cols] = highest
        tops[chunk:chunk + 1, cols] = highest
        peak[index] = highest

    def weight_strip(index, at, count):
        chunk, head = steps[index]
        start = CHUNKS[chunk][0] + at
        p_buf[start:start + count, head_cols(head)] = jnp.exp2(
            s_buf[index % 2, at:at + count, :] - peak[index]
        ).astype(bf16)

    def gather_values(index):
        chunk, head = steps[index]
        cols = head_cols(head)
        start, count = CHUNKS[chunk]
        found = dot(vT[:, start:start + count], p_buf[start:start + count, cols])
        if chunk > 0:
            total[:, cols] = total[:, cols] * fade[index] + found[128:129]
            acc[:, cols] = acc[:, cols] * fade[index] + found[:128]
        else:
            total[:, cols] = found[128:129]
            acc[:, cols] = found[:128]

    for at, count in strips(CHUNKS[0][1]):
        score_strip(0, at, count)
    for index in range(len(steps)):
        finish_peak(index)
        now = strips(CHUNKS[steps[index][0]][1])
        later = []
        if index + 1 < len(steps):
            chunk = steps[index + 1][0]
            if chunk != steps[index][0]:
                before_chunk(chunk)
            later = strips(CHUNKS[chunk][1])
        for turn in range(max(len(now), len(later))):
            if turn < len(later):
                score_strip(index + 1, *later[turn])
            if turn < len(now):
                weight_strip(index, *now[turn])
            if turn == 0 and index > 0:
                gather_values(index - 1)
    gather_values(len(steps) - 1)

    for head in range(HEADS):
        cols = head_cols(head)
        inverse = 1.0 / total[:, cols]
        out = acc[:, cols] * inverse
        delta[:, cols] = jnp.sum(out * dT[:, cols].astype(f32), 0, keepdims=True)
        out_ref[:, head * 128:(head + 1) * 128] = out.T.astype(bf16)
        for chunk in range(len(CHUNKS)):
            factor[chunk:chunk + 1, cols] = jnp.exp2(tops[chunk:chunk + 1, cols] - top[:, cols]) * inverse

    def back(start, count, chunk, values):
        for head in range(HEADS):
            cols = head_cols(head)
            weights = p_buf[start:start + count, cols] * factor[chunk:chunk + 1, cols].astype(bf16)
            p_buf[start:start + count, cols] = weights
            d_weights = dot(values, dT[:, cols])
            d_buf[start:start + count, cols] = weights * (d_weights - delta[:, cols]).astype(bf16)
        rows = slice(start, start + count)
        return dot(d_buf[rows, :], qs[...]) * SCALE, dot(p_buf[rows, :], ds[...])

    def back_slot(slot):
        return back(SLOT[slot], OWN, CHUNK_OF_SLOT[slot], kv[slot, 1])

    def to_other(index, slot):
        dk, dv = back_slot(slot)
        sib_send[index, :, 0:128] = dk.astype(bf16)
        sib_send[index, :, 128:256] = dv.astype(bf16)
        landing = {0: 0, 1: 2, 2: 1, 3: 3}[index]
        sends.append(
            send(sib_send.at[index], sib_recv.at[landing], sib_s.at[index], sib_r.at[landing], {"ctx": other})
        )

    def hold(index, slot):
        dk, dv = back_slot(slot)
        keep[index, :, 0:128] = dk
        keep[index, :, 128:256] = dv

    def landed(buffer, sems, index):
        pltpu.make_async_remote_copy(
            src_ref=buffer.at[index], dst_ref=buffer.at[index], send_sem=sems.at[index], recv_sem=sems.at[index],
            device_id={"ctx": other}, device_id_type=MESH,
        ).wait_recv()

    def to_chip(index, peer, value):
        x_send[index] = value.astype(bf16)
        sends.append(send(x_send.at[index], x_recv.at[index], x_s.at[index], x_r.at[index], {"ctx": peer}))

    def pair_sum(index):
        landed(sib_recv, sib_r, index)
        return keep[index] + sib_recv[index].astype(f32)

    to_other(0, 7)
    hold(0, 6)
    to_other(1, 4)
    to_other(2, 5)
    to_chip(0, ahead, pair_sum(0))
    hold(2, 3)
    hold(1, 2)
    to_chip(1, behind, pair_sum(2))
    to_other(3, 1)
    landed(x_recv, x_r, 0)
    to_chip(2, ahead, pair_sum(1) + x_recv[0].astype(f32))
    hold(3, 0)

    dk, dv = back(0, TOKENS, 0, sv_ref[...])
    dsk_ref[...] = dk.astype(bf16)
    dsv_ref[...] = dv.astype(bf16)

    def queries_gradient(head):
        turned = dot(kT[...], d_buf[:, head_cols(head)]) * SCALE
        dq_ref[:, head * 128:(head + 1) * 128] = turned.T.astype(bf16)

    queries_gradient(0)
    queries_gradient(1)
    keep[3] = pair_sum(3)
    landed(x_recv, x_r, 1)
    landed(x_recv, x_r, 2)
    keep[3] = keep[3] + x_recv[1].astype(f32) + x_recv[2].astype(f32)
    for piece in range(8):
        y_send[piece] = keep[3, piece * PIECE:(piece + 1) * PIECE, :].astype(bf16)
    for step in range(1, 8):
        peer = (dp + step) % 8
        sends.append(send(y_send.at[peer], y_recv.at[step], y_s.at[step], y_r.at[step], {"dp": peer}))
    for head in range(2, HEADS):
        queries_gradient(head)
    mine = keep[3, pl.ds(pl.multiple_of(dp * PIECE, 8), PIECE), :]
    for step in range(1, 8):
        landed(y_recv, y_r, step)
        mine = mine + y_recv[step].astype(f32)
    dpk_ref[...] = mine[:, 0:128]
    dpv_ref[...] = mine[:, 128:256]
    for copy in sends:
        copy.wait_send()


def shards(queries, suffix_keys, suffix_values, pre_keys, pre_values, segments, d_out):
    vmem = pl.BlockSpec(memory_space=pltpu.VMEM)
    dma = pltpu.SemaphoreType.DMA
    return pl.pallas_call(
        kernel,
        out_shape=[
            jax.ShapeDtypeStruct((TOKENS, HEADS * HEAD_WIDTH), bf16),
            jax.ShapeDtypeStruct((TOKENS, HEADS * HEAD_WIDTH), bf16),
            jax.ShapeDtypeStruct((TOKENS, HEAD_WIDTH), bf16),
            jax.ShapeDtypeStruct((TOKENS, HEAD_WIDTH), bf16),
            jax.ShapeDtypeStruct((PIECE, HEAD_WIDTH), f32),
            jax.ShapeDtypeStruct((PIECE, HEAD_WIDTH), f32),
        ],
        in_specs=[vmem] * 7,
        out_specs=[vmem] * 6,
        scratch_shapes=[
            pltpu.VMEM((8, 2, OWN, HEAD_WIDTH), bf16),
            pltpu.VMEM((256, ROWS), bf16),
            pltpu.VMEM((128, ROWS), bf16),
            pltpu.VMEM((ROWS, HEAD_WIDTH), bf16),
            pltpu.VMEM((ROWS, HEAD_WIDTH), bf16),
            pltpu.VMEM((128, KEYS), bf16),
            pltpu.VMEM((144, KEYS), bf16),
            pltpu.VMEM((KEYS, 256), bf16),
            pltpu.VMEM((TOKENS, TOKENS), f32),
            pltpu.VMEM((1, ROWS), f32),
            pltpu.VMEM((1, ROWS), f32),
            pltpu.VMEM((128, ROWS), f32),
            pltpu.VMEM((8, ROWS), f32),
            pltpu.VMEM((1, ROWS), f32),
            pltpu.VMEM((8, ROWS), f32),
            pltpu.VMEM((2, 768, TOKENS), f32),
            pltpu.VMEM((KEYS, ROWS), bf16),
            pltpu.VMEM((KEYS, ROWS), bf16),
            pltpu.VMEM((4, OWN, 256), f32),
            pltpu.VMEM((4, OWN, 256), bf16),
            pltpu.VMEM((4, OWN, 256), bf16),
            pltpu.VMEM((3, OWN, 256), bf16),
            pltpu.VMEM((3, OWN, 256), bf16),
            pltpu.VMEM((8, PIECE, 256), bf16),
            pltpu.VMEM((8, PIECE, 256), bf16),
            dma((7,)), dma((8,)), dma((4,)), dma((4,)), dma((3,)), dma((3,)), dma((8,)), dma((8,)),
        ],
        compiler_params=pltpu.CompilerParams(
            collective_id=0, has_side_effects=True, vmem_limit_bytes=60 << 20
        ),
    )(queries, suffix_keys, suffix_values, pre_keys, pre_values, segments, d_out)


def solution(mesh):
    split = P(("ctx", "dp"), "mp")
    in_specs = (split, split, split, P("ctx", "mp"), P("ctx", "mp"), P(("ctx", "dp"), None), split)
    return jax.shard_map(shards, mesh=mesh, in_specs=in_specs, out_specs=(split,) * 6, check_vma=False)
```

time: 300 us -> 49.9 us (0.17)
  the two profiles are of different devices: /device:TPU:6 before, /device:TPU:2 now
where the time goes in v1:
time: 49.9 us; the launch traced here: 49.5 us
  Pallas kernels  43.3 us (87%)
  local copies, waits for them, and re-layouts  5.59 us (11%)
  between operations  0.66 us (1%)
    pallas_call x1, Pallas kernels, shards(): pl.pallas_call(kernel, out_shape=[jax.ShapeDtypeStruct((TOKENS, HEADS * H...  43.3 us
    unnamed x16, local copies, waits for them, and re-layouts  5.59 us

profile of v1, /device:TPU:2, one launch (start us, length us, event | category | flops | bytes accessed | tf_op | source)
XLA Modules:
  0.0 49.5 jit_solution(1965701552484889202)
XLA Ops:
  0.6 43.3 %shard_map.118 = (bf16[256,640]{1,0:T(8,128)(2,1)}, bf16[256,640]{1,0:T(8,128)(2,1)}, bf16[256,128]{1,0:T(8,128)(2,1)}, bf16[256,128]{1,0:T(8,128)(2,1)}, f32[48,128]{1,0:T(8,128)}, /*index=5*/f32[48,128]{1,0:T(8,128)}) custom-call(bf16[256,640]{1,0:T(8,128)(2,1)} %q_ref.1, bf16[256,128]{1,0:T(8,128)(2,1)} %sk_ref.1, bf16[256,128]{1,0:T(8,128)(2,1)} %sv_ref.1, ...), custom_call_target="tpu_custom_call" | custom-call | tf_op jit(solution)/shard_map/pallas_call | solution.py:297
  43.9 0.0 copy-start
  43.9 1.8 %copy.19 = bf16[256,640]{1,0:T(8,128)(2,1)} copy(bf16[256,640]{1,0:T(8,128)(2,1)} %get-tuple-element.12) | data formatting | bytes 655360
  45.7 0.0 copy-done
  45.7 0.0 copy-start.2
  45.7 0.7 %copy.20 = bf16[256,640]{1,0:T(8,128)(2,1)} copy(bf16[256,640]{1,0:T(8,128)(2,1)S(1)} %copy-done) | data formatting | bytes 655360
  46.4 0.1 copy-done.2
  46.5 0.0 copy-start.1
  46.6 0.6 %copy.21 = bf16[256,128]{1,0:T(8,128)(2,1)} copy(bf16[256,128]{1,0:T(8,128)(2,1)S(1)} %copy-done.2) | data formatting | bytes 131072
  47.2 0.2 copy-done.1
  47.4 0.0 copy-start.4
  47.4 0.6 %copy.22 = bf16[256,128]{1,0:T(8,128)(2,1)} copy(bf16[256,128]{1,0:T(8,128)(2,1)S(1)} %copy-done.1) | data formatting | bytes 131072
  48.0 0.1 copy-done.4
  48.2 0.0 copy-start.3
  48.2 0.6 %copy.23 = f32[48,128]{1,0:T(8,128)} copy(f32[48,128]{1,0:T(8,128)S(1)} %copy-done.4) | data formatting | bytes 49152
  48.8 0.1 copy-done.3
  48.9 0.6 %copy.24 = f32[48,128]{1,0:T(8,128)} copy(f32[48,128]{1,0:T(8,128)S(1)} %copy-done.3) | data formatting | bytes 49152
Async XLA Ops:
  43.9 1.8 %copy-start = (bf16[256,640]{1,0:T(8,128)(2,1)S(1)}, bf16[256,640]{1,0:T(8,128)(2,1)}, u32[]{:S(2)}) copy-start(bf16[256,640]{1,0:T(8,128)(2,1)} %get-tuple-element.13) | copy-start | bytes 983044
  45.7 0.9 %copy-start.2 = (bf16[256,128]{1,0:T(8,128)(2,1)S(1)}, bf16[256,128]{1,0:T(8,128)(2,1)}, u32[]{:S(2)}) copy-start(bf16[256,128]{1,0:T(8,128)(2,1)} %get-tuple-element.14) | copy-start | bytes 196612
  46.5 0.9 %copy-start.1 = (bf16[256,128]{1,0:T(8,128)(2,1)S(1)}, bf16[256,128]{1,0:T(8,128)(2,1)}, u32[]{:S(2)}) copy-start(bf16[256,128]{1,0:T(8,128)(2,1)} %get-tuple-element.15) | copy-start | bytes 196612
  47.4 0.7 %copy-start.4 = (f32[48,128]{1,0:T(8,128)S(1)}, f32[48,128]{1,0:T(8,128)}, u32[]{:S(2)}) copy-start(f32[48,128]{1,0:T(8,128)} %get-tuple-element.16) | copy-start | bytes 73732
  48.2 0.7 %copy-start.3 = (f32[48,128]{1,0:T(8,128)S(1)}, f32[48,128]{1,0:T(8,128)}, u32[]{:S(2)}) copy-start(f32[48,128]{1,0:T(8,128)} %get-tuple-element.17) | copy-start | bytes 73732

commit v2 on v1

v2 whole, which is shorter than its diff:
```python
import jax
import jax.numpy as jnp
from jax import lax
from jax.experimental import pallas as pl
from jax.experimental.pallas import tpu as pltpu
from jax.sharding import PartitionSpec as P

HEAD_WIDTH = 128
HEADS = 5
TOKENS = 256
ROWS = HEADS * TOKENS
OWN = 384
PIECE = 48
SCALE = HEAD_WIDTH ** (-0.5)
LOG2_SCALE = 1.4426950408889634 * SCALE
MESH = pl.DeviceIdType.MESH
bf16 = jnp.bfloat16
f32 = jnp.float32

PART = 128
PARTS = 3
ARRIVALS = [
    [(0, 0), (0, 1), (0, 2)],
    [(1, 0), (1, 1), (1, 2)],
    [(2, 0), (3, 0)],
    [(2, 1), (3, 1), (4, 0), (5, 0)],
    [(2, 2), (3, 2), (4, 1), (5, 1), (6, 0)],
    [(4, 2), (5, 2), (6, 1), (7, 0)],
    [(6, 2), (7, 1), (7, 2)],
]
KEYS = TOKENS + 8 * OWN
START, CHUNK_OF, CHUNKS = {}, {}, []
for chunk, arriving in enumerate(ARRIVALS):
    begin = 0 if chunk == 0 else sum(CHUNKS[-1])
    at = TOKENS if chunk == 0 else begin
    for place in arriving:
        START[place], CHUNK_OF[place] = at, chunk
        at += PART
    CHUNKS.append((begin, at - begin))
STRIP = 256
LANDING = {0: 0, 1: 2, 2: 1, 3: 3}


def dot(left, right):
    return lax.dot_general(left, right, (((1,), (0,)), ((), ())), preferred_element_type=f32)


def head_cols(head):
    return slice(head * TOKENS, (head + 1) * TOKENS)


def strips(count):
    return [(at, min(STRIP, count - at)) for at in range(0, count, STRIP)]


def kernel(
    q_ref, sk_ref, sv_ref, pk_ref, pv_ref, seg_ref, do_ref,
    out_ref, dq_ref, dsk_ref, dsv_ref, dpk_ref, dpv_ref,
    q_v, sk_v, sv_v, pk_v, pv_v, seg_v, do_v, out_v, dq_v, dsk_v, dsv_v, dpk_v, dpv_v,
    kv, qT, dT, qs, ds, kT, vT, k2, bias, top, total, acc, tops, delta, factor, s_buf, p_buf, d_buf,
    keep, sib_send, sib_recv, x_send, x_recv, y_send, y_recv,
    in_s, out_s, ag_s, ag_r, sib_s, sib_r, x_s, x_r, y_s, y_r,
):
    ctx = lax.axis_index("ctx")
    dp = lax.axis_index("dp")
    core = ctx % 2
    chip = ctx // 2
    ahead = ((chip + 1 + 2 * core) % 4) * 2 + core
    behind = ((chip + 3 + 2 * core) % 4) * 2 + core
    other = chip * 2 + (1 - core)

    barrier = pltpu.get_barrier_semaphore()
    for peer in (ahead, behind, other):
        pl.semaphore_signal(barrier, inc=1, device_id={"ctx": peer}, device_id_type=MESH)
    for step in range(1, 8):
        pl.semaphore_signal(barrier, inc=1, device_id={"dp": (dp + step) % 8}, device_id_type=MESH)

    loads = {}
    for index, (name, source, target) in enumerate((
        ("pk", pk_ref, pk_v), ("pv", pv_ref, pv_v), ("q", q_ref, q_v), ("seg", seg_ref, seg_v),
        ("sk", sk_ref, sk_v), ("sv", sv_ref, sv_v), ("do", do_ref, do_v),
    )):
        loads[name] = pltpu.make_async_copy(source, target, in_s.at[index])
        loads[name].start()
    stores = []

    def store(source, target):
        copy = pltpu.make_async_copy(source, target, out_s.at[len(stores)])
        copy.start()
        stores.append(copy)

    sends = []

    def send(src, dst, s_sem, r_sem, device):
        copy = pltpu.make_async_remote_copy(
            src_ref=src, dst_ref=dst, send_sem=s_sem, recv_sem=r_sem, device_id=device, device_id_type=MESH
        )
        copy.start()
        sends.append(copy)

    counter = []

    def spread(source, slot, part, peer):
        index = len(counter)
        counter.append(0)
        send(kv.at[source, part], kv.at[slot, part], ag_s.at[index], ag_r.at[slot, part], {"ctx": peer})

    def arrived(slot, part):
        pltpu.make_async_remote_copy(
            src_ref=kv.at[slot, part], dst_ref=kv.at[slot, part], send_sem=ag_s.at[0], recv_sem=ag_r.at[slot, part],
            device_id={"ctx": other}, device_id_type=MESH,
        ).wait_recv()

    def prepare_keys(start, keys, values):
        count = keys.shape[0]
        kT[:, start:start + count] = keys.T
        vT[0:128, start:start + count] = values.T
        scaled = keys.astype(f32) * LOG2_SCALE
        high = scaled.astype(bf16)
        k2[start:start + count, 0:128] = high
        k2[start:start + count, 128:256] = (scaled - high.astype(f32)).astype(bf16)

    def ready(slot, part):
        prepare_keys(START[slot, part], kv[slot, part, 0], kv[slot, part, 1])

    loads["pk"].wait()
    loads["pv"].wait()
    for part in range(PARTS):
        for owner in range(8):
            rows = slice(owner * PIECE + part * 16, owner * PIECE + part * 16 + 16)
            kv[0, part, 0, owner * 16:owner * 16 + 16, :] = pk_v[rows, :]
            kv[0, part, 1, owner * 16:owner * 16 + 16, :] = pv_v[rows, :]
    pl.semaphore_wait(barrier, 10)
    for part in range(PARTS):
        spread(0, 3, part, ahead)
        spread(0, 2, part, behind)
        spread(0, 1, part, other)

    loads["q"].wait()
    loads["seg"].wait()
    loads["sk"].wait()
    loads["sv"].wait()
    loads["do"].wait()
    for head in range(HEADS):
        cols = head_cols(head)
        width = slice(head * 128, (head + 1) * 128)
        q_head, do_head = q_v[:, width], do_v[:, width]
        q_turned = q_head.T
        qT[0:128, cols] = q_turned
        qT[128:256, cols] = q_turned
        dT[:, cols] = do_head.T
        qs[cols, :] = q_head
        ds[cols, :] = do_head
    seg = jnp.broadcast_to(seg_v[...].astype(f32), (TOKENS, TOKENS))
    key_id = lax.broadcasted_iota(jnp.int32, (TOKENS, TOKENS), 0)
    token_id = lax.broadcasted_iota(jnp.int32, (TOKENS, TOKENS), 1)
    bias[...] = jnp.where((seg == seg.T) & (key_id <= token_id), 0.0, -1e30)
    vT[128:144, :] = jnp.where(lax.broadcasted_iota(jnp.int32, (16, KEYS), 0) == 0, 1.0, 0.0).astype(bf16)
    prepare_keys(0, sk_v[...], sv_v[...])
    for part in range(PARTS):
        ready(0, part)

    def before_chunk(chunk):
        for slot, part in ARRIVALS[chunk]:
            if slot == 3:
                arrived(3, part)
                spread(3, 6, part, ahead)
                spread(3, 4, part, other)
            if slot == 2:
                arrived(2, part)
                spread(2, 5, part, other)
            if slot == 6:
                arrived(6, part)
                spread(6, 7, part, other)
        for slot, part in ARRIVALS[chunk]:
            if slot in (1, 4, 5, 7):
                arrived(slot, part)
            ready(slot, part)

    steps = [(chunk, head) for chunk in range(len(CHUNKS)) for head in range(HEADS)]
    peak, fade = {}, {}

    def score_strip(index, at, count):
        chunk, head = steps[index]
        start = CHUNKS[chunk][0] + at
        s = dot(k2[start:start + count, :], qT[:, head_cols(head)])
        if chunk == 0 and at < TOKENS:
            s = s + bias[at:at + count, :]
        s_buf[index % 2, at:at + count, :] = s
        part = jnp.max(s.reshape(count // 8, 8, TOKENS), 0)
        peak[index] = part if index not in peak else jnp.maximum(peak[index], part)

    def finish_peak(index):
        chunk, head = steps[index]
        cols = head_cols(head)
        highest = jnp.max(peak[index], 0, keepdims=True)
        if chunk > 0:
            before = top[:, cols]
            highest = jnp.maximum(highest, before)
            fade[index] = jnp.exp2(before - highest)
        top[:, cols] = highest
        tops[chunk:chunk + 1, cols] = highest
        peak[index] = highest

    def weight_strip(index, at, count):
        chunk, head = steps[index]
        start = CHUNKS[chunk][0] + at
        p_buf[start:start + count, head_cols(head)] = jnp.exp2(
            s_buf[index % 2, at:at + count, :] - peak[index]
        ).astype(bf16)

    def gather_values(index):
        chunk, head = steps[index]
        cols = head_cols(head)
        start, count = CHUNKS[chunk]
        found = dot(vT[:, start:start + count], p_buf[start:start + count, cols])
        if chunk > 0:
            total[:, cols] = total[:, cols] * fade[index] + found[128:129]
            acc[:, cols] = acc[:, cols] * fade[index] + found[:128]
        else:
            total[:, cols] = found[128:129]
            acc[:, cols] = found[:128]

    for at, count in strips(CHUNKS[0][1]):
        score_strip(0, at, count)
    for index in range(len(steps)):
        finish_peak(index)
        now = strips(CHUNKS[steps[index][0]][1])
        later = []
        if index + 1 < len(steps):
            chunk = steps[index + 1][0]
            if chunk != steps[index][0]:
                before_chunk(chunk)
            later = strips(CHUNKS[chunk][1])
        for turn in range(max(len(now), len(later))):
            if turn < len(later):
                score_strip(index + 1, *later[turn])
            if turn < len(now):
                weight_strip(index, *now[turn])
            if turn == 0 and index > 0:
                gather_values(index - 1)
    gather_values(len(steps) - 1)

    for head in range(HEADS):
        cols = head_cols(head)
        inverse = 1.0 / total[:, cols]
        out = acc[:, cols] * inverse
        delta[:, cols] = jnp.sum(out * dT[:, cols].astype(f32), 0, keepdims=True)
        out_v[:, head * 128:(head + 1) * 128] = out.T.astype(bf16)
        for chunk in range(len(CHUNKS)):
            factor[chunk:chunk + 1, cols] = jnp.exp2(tops[chunk:chunk + 1, cols] - top[:, cols]) * inverse

    store(out_v, out_ref)

    def back(start, count, chunk, values):
        for head in range(HEADS):
            cols = head_cols(head)
            weights = p_buf[start:start + count, cols] * factor[chunk:chunk + 1, cols].astype(bf16)
            p_buf[start:start + count, cols] = weights
            d_weights = dot(values, dT[:, cols])
            d_buf[start:start + count, cols] = weights * (d_weights - delta[:, cols]).astype(bf16)
        rows = slice(start, start + count)
        return dot(d_buf[rows, :], qs[...]) * SCALE, dot(p_buf[rows, :], ds[...])

    def back_part(slot, part):
        return back(START[slot, part], PART, CHUNK_OF[slot, part], kv[slot, part, 1])

    def for_other(index, part, slot):
        dk, dv = back_part(slot, part)
        sib_send[index, part, :, 0:128] = dk.astype(bf16)
        sib_send[index, part, :, 128:256] = dv.astype(bf16)

    def hold(index, part, slot):
        dk, dv = back_part(slot, part)
        keep[index, part, :, 0:128] = dk
        keep[index, part, :, 128:256] = dv

    def to_other(*places):
        for index, part in places:
            landing = LANDING[index]
            send(
                sib_send.at[index, part], sib_recv.at[landing, part], sib_s.at[index, part], sib_r.at[landing, part],
                {"ctx": other},
            )

    def landed(buffer, sems, index, part):
        pltpu.make_async_remote_copy(
            src_ref=buffer.at[index, part], dst_ref=buffer.at[index, part],
            send_sem=sems.at[index, part], recv_sem=sems.at[index, part],
            device_id={"ctx": other}, device_id_type=MESH,
        ).wait_recv()

    def to_chips(*places):
        for index, part in places:
            landed(sib_recv, sib_r, (0, 2, 1)[index], part)
            if index == 2:
                landed(x_recv, x_r, 0, part)
        for index, part in places:
            row = (0, 2, 1)[index]
            value = keep[row, part] + sib_recv[row, part].astype(f32)
            if index == 2:
                value = value + x_recv[0, part].astype(f32)
            x_send[index, part] = value.astype(bf16)
        for index, part in places:
            peer = behind if index == 1 else ahead
            send(x_send.at[index, part], x_recv.at[index, part], x_s.at[index, part], x_r.at[index, part], {"ctx": peer})

    def opposite(part):
        for_other(0, part, 7)
        hold(0, part, 6)

    def sides_other(part):
        for_other(1, part, 4)
        for_other(2, part, 5)

    def sides_same(part):
        hold(2, part, 3)
        hold(1, part, 2)

    def own(part):
        for_other(3, part, 1)
        hold(3, part, 0)

    def exchange(part):
        landed(sib_recv, sib_r, 3, part)
        landed(x_recv, x_r, 1, part)
        landed(x_recv, x_r, 2, part)
        mine = keep[3, part] + sib_recv[3, part].astype(f32)
        mine = mine + x_recv[1, part].astype(f32) + x_recv[2, part].astype(f32)
        keep[3, part] = mine
        for owner in range(8):
            y_send[part, owner] = mine[owner * 16:owner * 16 + 16, :].astype(bf16)
        for step in (4, 3, 5, 2, 6, 1, 7):
            peer = (dp + step) % 8
            send(y_send.at[part, peer], y_recv.at[part, step], y_s.at[part, step], y_r.at[part, step], {"dp": peer})

    def finish(part):
        for step in range(1, 8):
            landed(y_recv, y_r, part, step)
        mine = keep[3, part, pl.ds(pl.multiple_of(dp * 16, 16), 16), :]
        for step in range(1, 8):
            mine = mine + y_recv[part, step].astype(f32)
        dpk_v[part * 16:part * 16 + 16, :] = mine[:, 0:128]
        dpv_v[part * 16:part * 16 + 16, :] = mine[:, 128:256]

    def own_keys():
        dk, dv = back(0, TOKENS, 0, sv_v[...])
        dsk_v[...] = dk.astype(bf16)
        dsv_v[...] = dv.astype(bf16)

    def queries_gradient(head):
        turned = dot(kT[...], d_buf[:, head_cols(head)]) * SCALE
        dq_v[:, head * 128:(head + 1) * 128] = turned.T.astype(bf16)

    opposite(0)
    opposite(1)
    to_other((0, 0), (0, 1))
    opposite(2)
    sides_other(0)
    to_other((0, 2), (1, 0), (2, 0))
    to_chips((0, 0), (0, 1))
    sides_same(0)
    sides_other(1)
    to_other((1, 1), (2, 1))
    to_chips((0, 2), (1, 0))
    sides_same(1)
    sides_other(2)
    to_other((1, 2), (2, 2))
    to_chips((1, 1))
    sides_same(2)
    own(0)
    to_other((3, 0))
    to_chips((1, 2), (2, 0))
    own(1)
    own(2)
    to_other((3, 1), (3, 2))
    to_chips((2, 1), (2, 2))
    own_keys()
    for head in range(HEADS):
        queries_gradient(head)
    store(dsk_v, dsk_ref)
    store(dsv_v, dsv_ref)
    store(dq_v, dq_ref)
    for part in range(PARTS):
        exchange(part)
    for part in range(PARTS):
        finish(part)
    store(dpk_v, dpk_ref)
    store(dpv_v, dpv_ref)
    for copy in sends:
        copy.wait_send()
    for copy in stores:
        copy.wait()


def hand_over(*refs):
    sources, targets, held, (in_s, out_s) = refs[:6], refs[6:12], refs[12:18], refs[18:]
    loads = [pltpu.make_async_copy(sources[i], held[i], in_s.at[i]) for i in range(6)]
    stores = [pltpu.make_async_copy(held[i], targets[i], out_s.at[i]) for i in range(6)]
    for load in loads:
        load.start()
    for load, store in zip(loads, stores):
        load.wait()
        store.start()
    for store in stores:
        store.wait()


def shards(queries, suffix_keys, suffix_values, pre_keys, pre_values, segments, d_out):
    anywhere = pl.BlockSpec(memory_space=pl.ANY)
    dma = pltpu.SemaphoreType.DMA
    shapes = [
        ((TOKENS, HEADS * HEAD_WIDTH), bf16),
        ((TOKENS, HEADS * HEAD_WIDTH), bf16),
        ((TOKENS, HEAD_WIDTH), bf16),
        ((TOKENS, HEAD_WIDTH), bf16),
        ((PIECE, HEAD_WIDTH), f32),
        ((PIECE, HEAD_WIDTH), f32),
    ]
    out_shape = [jax.ShapeDtypeStruct(shape, dtype) for shape, dtype in shapes]
    results = pl.pallas_call(
        kernel,
        out_shape=out_shape,
        in_specs=[anywhere] * 7,
        out_specs=[anywhere] * 6,
        scratch_shapes=[
            pltpu.VMEM((TOKENS, HEADS * HEAD_WIDTH), bf16),
            pltpu.VMEM((TOKENS, HEAD_WIDTH), bf16),
            pltpu.VMEM((TOKENS, HEAD_WIDTH), bf16),
            pltpu.VMEM((OWN, HEAD_WIDTH), bf16),
            pltpu.VMEM((OWN, HEAD_WIDTH), bf16),
            pltpu.VMEM((1, TOKENS), jnp.int32),
            pltpu.VMEM((TOKENS, HEADS * HEAD_WIDTH), bf16),
        ] + [pltpu.VMEM(shape, dtype) for shape, dtype in shapes] + [
            pltpu.VMEM((8, PARTS, 2, PART, HEAD_WIDTH), bf16),
            pltpu.VMEM((256, ROWS), bf16),
            pltpu.VMEM((128, ROWS), bf16),
            pltpu.VMEM((ROWS, HEAD_WIDTH), bf16),
            pltpu.VMEM((ROWS, HEAD_WIDTH), bf16),
            pltpu.VMEM((128, KEYS), bf16),
            pltpu.VMEM((144, KEYS), bf16),
            pltpu.VMEM((KEYS, 256), bf16),
            pltpu.VMEM((TOKENS, TOKENS), f32),
            pltpu.VMEM((1, ROWS), f32),
            pltpu.VMEM((1, ROWS), f32),
            pltpu.VMEM((128, ROWS), f32),
            pltpu.VMEM((8, ROWS), f32),
            pltpu.VMEM((1, ROWS), f32),
            pltpu.VMEM((8, ROWS), f32),
            pltpu.VMEM((2, 768, TOKENS), f32),
            pltpu.VMEM((KEYS, ROWS), bf16),
            pltpu.VMEM((KEYS, ROWS), bf16),
            pltpu.VMEM((4, PARTS, PART, 256), f32),
            pltpu.VMEM((4, PARTS, PART, 256), bf16),
            pltpu.VMEM((4, PARTS, PART, 256), bf16),
            pltpu.VMEM((3, PARTS, PART, 256), bf16),
            pltpu.VMEM((3, PARTS, PART, 256), bf16),
            pltpu.VMEM((PARTS, 8, 16, 256), bf16),
            pltpu.VMEM((PARTS, 8, 16, 256), bf16),
            dma((7,)), dma((10,)), dma((21,)), dma((8, PARTS)), dma((4, PARTS)), dma((4, PARTS)),
            dma((3, PARTS)), dma((3, PARTS)), dma((PARTS, 8)), dma((PARTS, 8)),
        ],
        compiler_params=pltpu.CompilerParams(
            collective_id=0, has_side_effects=True, vmem_limit_bytes=60 << 20
        ),
    )(queries, suffix_keys, suffix_values, pre_keys, pre_values, segments, d_out)
    return pl.pallas_call(
        hand_over,
        out_shape=out_shape,
        in_specs=[anywhere] * 6,
        out_specs=[anywhere] * 6,
        scratch_shapes=[pltpu.VMEM(shape, dtype) for shape, dtype in shapes] + [dma((6,)), dma((6,))],
    )(*results)


def solution(mesh):
    split = P(("ctx", "dp"), "mp")
    in_specs = (split, split, split, P("ctx", "mp"), P("ctx", "mp"), P(("ctx", "dp"), None), split)
    return jax.shard_map(shards, mesh=mesh, in_specs=in_specs, out_specs=(split,) * 6, check_vma=False)
```

time: 49.9 us -> 45.6 us (0.914)
  the two profiles are of different devices: /device:TPU:2 before, /device:TPU:1 now
where the time goes in v2:
time: 45.6 us; the launch traced here: 45.4 us
  Pallas kernels  44.6 us (98%)
  between operations  0.8 us (2%)
    pallas_call x1, Pallas kernels, shards(): pl.pallas_call(kernel, out_shape=out_shape, in_specs=[anywhere] * 7, out_...  42.7 us
    pallas_call x1, Pallas kernels, shards(): pl.pallas_call(hand_over, out_shape=out_shape, in_specs=[anywhere] * 6, o...  1.95 us

profile of v2, /device:TPU:1, one launch (start us, length us, event | category | flops | bytes accessed | tf_op | source)
XLA Modules:
  0.0 45.4 jit_solution(5537352793592269303)
XLA Ops:
  0.6 42.7 %shard_map.118 = (bf16[256,640]{1,0:T(8,128)(2,1)}, bf16[256,640]{1,0:T(8,128)(2,1)}, bf16[256,128]{1,0:T(8,128)(2,1)}, bf16[256,128]{1,0:T(8,128)(2,1)}, f32[48,128]{1,0:T(8,128)}, /*index=5*/f32[48,128]{1,0:T(8,128)}) custom-call(bf16[256,640]{1,0:T(8,128)(2,1)} %q_ref.1, bf16[256,128]{1,0:T(8,128)(2,1)} %sk_ref.1, bf16[256,128]{1,0:T(8,128)(2,1)} %sv_ref.1, ...), custom_call_target="tpu_custom_call" | custom-call | tf_op jit(solution)/shard_map/pallas_call | solution.py:421
  43.3 2.0 %shard_map.119 = (bf16[256,640]{1,0:T(8,128)(2,1)}, bf16[256,640]{1,0:T(8,128)(2,1)}, bf16[256,128]{1,0:T(8,128)(2,1)}, bf16[256,128]{1,0:T(8,128)(2,1)}, f32[48,128]{1,0:T(8,128)}, /*index=5*/f32[48,128]{1,0:T(8,128)}) custom-call(bf16[256,640]{1,0:T(8,128)(2,1)} %get-tuple-element.12.refs_0_, bf16[256,640]{1,0:T(8,128)(2,1)} %get-tuple-element.13.refs_1_, ...), custom_call_target="tpu_custom_call" | custom-call | tf_op jit(solution)/shard_map/pallas_call | solution.py:467

commit v3 on v2

--- a/solution.py
+++ b/solution.py
@@ -22,10 +22,10 @@
 ARRIVALS = [
     [(0, 0), (0, 1), (0, 2)],
     [(1, 0), (1, 1), (1, 2)],
-    [(2, 0), (3, 0)],
-    [(2, 1), (3, 1), (4, 0), (5, 0)],
-    [(2, 2), (3, 2), (4, 1), (5, 1), (6, 0)],
-    [(4, 2), (5, 2), (6, 1), (7, 0)],
+    [(2, 1), (3, 1)],
+    [(2, 2), (3, 2), (4, 1), (5, 1)],
+    [(2, 0), (3, 0), (6, 0), (4, 2), (5, 2)],
+    [(4, 0), (5, 0), (6, 1), (7, 0)],
     [(6, 2), (7, 1), (7, 2)],
 ]
 KEYS = TOKENS + 8 * OWN
@@ -56,10 +56,10 @@
 def kernel(
     q_ref, sk_ref, sv_ref, pk_ref, pv_ref, seg_ref, do_ref,
     out_ref, dq_ref, dsk_ref, dsv_ref, dpk_ref, dpv_ref,
-    q_v, sk_v, sv_v, pk_v, pv_v, seg_v, do_v, out_v, dq_v, dsk_v, dsv_v, dpk_v, dpv_v,
-    kv, qT, dT, qs, ds, kT, vT, k2, bias, top, total, acc, tops, delta, factor, s_buf, p_buf, d_buf,
+    q_v, sk_v, sv_v, pk_v, pv_v, seg_v, do_v,
+    kv, qT, dT, qs, ds, kT, vT, k2, bias, top, total, acc, tops, delta, factor, s_buf, p_buf, d_buf, vn, g_buf,
     keep, sib_send, sib_recv, x_send, x_recv, y_send, y_recv,
-    in_s, out_s, ag_s, ag_r, sib_s, sib_r, x_s, x_r, y_s, y_r,
+    in_s, ag_s, ag_r, sib_s, sib_r, x_s, x_r, y_s, y_r,
 ):
     ctx = lax.axis_index("ctx")
     dp = lax.axis_index("dp")
@@ -67,10 +67,11 @@
     chip = ctx // 2
     ahead = ((chip + 1 + 2 * core) % 4) * 2 + core
     behind = ((chip + 3 + 2 * core) % 4) * 2 + core
+    opposite_chip = ((chip + 2) % 4) * 2 + core
     other = chip * 2 + (1 - core)
 
     barrier = pltpu.get_barrier_semaphore()
-    for peer in (ahead, behind, other):
+    for peer in (ahead, behind, opposite_chip, other):
         pl.semaphore_signal(barrier, inc=1, device_id={"ctx": peer}, device_id_type=MESH)
     for step in range(1, 8):
         pl.semaphore_signal(barrier, inc=1, device_id={"dp": (dp + step) % 8}, device_id_type=MESH)
@@ -82,13 +83,6 @@
     )):
         loads[name] = pltpu.make_async_copy(source, target, in_s.at[index])
         loads[name].start()
-    stores = []
-
-    def store(source, target):
-        copy = pltpu.make_async_copy(source, target, out_s.at[len(stores)])
-        copy.start()
-        stores.append(copy)
-
     sends = []
 
     def send(src, dst, s_sem, r_sem, device):
@@ -115,6 +109,7 @@
         count = keys.shape[0]
         kT[:, start:start + count] = keys.T
         vT[0:128, start:start + count] = values.T
+        vn[start:start + count, :] = values
         scaled = keys.astype(f32) * LOG2_SCALE
         high = scaled.astype(bf16)
         k2[start:start + count, 0:128] = high
@@ -130,8 +125,10 @@
             rows = slice(owner * PIECE + part * 16, owner * PIECE + part * 16 + 16)
             kv[0, part, 0, owner * 16:owner * 16 + 16, :] = pk_v[rows, :]
             kv[0, part, 1, owner * 16:owner * 16 + 16, :] = pv_v[rows, :]
-    pl.semaphore_wait(barrier, 10)
-    for part in range(PARTS):
+    pl.semaphore_wait(barrier, 11)
+    for part in (1, 2, 0):
+        if part == 0:
+            spread(0, 6, part, opposite_chip)
         spread(0, 3, part, ahead)
         spread(0, 2, part, behind)
         spread(0, 1, part, other)
@@ -164,12 +161,13 @@
         for slot, part in ARRIVALS[chunk]:
             if slot == 3:
                 arrived(3, part)
-                spread(3, 6, part, ahead)
+                if part > 0:
+                    spread(3, 6, part, ahead)
                 spread(3, 4, part, other)
             if slot == 2:
                 arrived(2, part)
                 spread(2, 5, part, other)
-            if slot == 6:
+            if slot == 6 and part == 0:
                 arrived(6, part)
                 spread(6, 7, part, other)
         for slot, part in ARRIVALS[chunk]:
@@ -220,6 +218,11 @@
         else:
             total[:, cols] = found[128:129]
             acc[:, cols] = found[:128]
+
+    def weight_gradients(index):
+        chunk, head = steps[index]
+        start, count = CHUNKS[chunk]
+        g_buf[start:start + count, head_cols(head)] = dot(vn[start:start + count, :], dT[:, head_cols(head)])
 
     for at, count in strips(CHUNKS[0][1]):
         score_strip(0, at, count)
@@ -239,6 +242,11 @@
                 weight_strip(index, *now[turn])
             if turn == 0 and index > 0:
                 gather_values(index - 1)
+        weight_gradients(index)
+        if steps[index] in ((4, 1), (5, 1)):
+            part = steps[index][0] - 3
+            arrived(6, part)
+            spread(6, 7, part, other)
     gather_values(len(steps) - 1)
 
     for head in range(HEADS):
@@ -246,24 +254,22 @@
         inverse = 1.0 / total[:, cols]
         out = acc[:, cols] * inverse
         delta[:, cols] = jnp.sum(out * dT[:, cols].astype(f32), 0, keepdims=True)
-        out_v[:, head * 128:(head + 1) * 128] = out.T.astype(bf16)
+        acc[:, cols] = out
         for chunk in range(len(CHUNKS)):
             factor[chunk:chunk + 1, cols] = jnp.exp2(tops[chunk:chunk + 1, cols] - top[:, cols]) * inverse
 
-    store(out_v, out_ref)
-
-    def back(start, count, chunk, values):
+    def back(start, count, chunk):
         for head in range(HEADS):
             cols = head_cols(head)
             weights = p_buf[start:start + count, cols] * factor[chunk:chunk + 1, cols].astype(bf16)
             p_buf[start:start + count, cols] = weights
-            d_weights = dot(values, dT[:, cols])
+            d_weights = g_buf[start:start + count, cols]
             d_buf[start:start + count, cols] = weights * (d_weights - delta[:, cols]).astype(bf16)
         rows = slice(start, start + count)
         return dot(d_buf[rows, :], qs[...]) * SCALE, dot(p_buf[rows, :], ds[...])
 
     def back_part(slot, part):
-        return back(START[slot, part], PART, CHUNK_OF[slot, part], kv[slot, part, 1])
+        return back(START[slot, part], PART, CHUNK_OF[slot, part])
 
     def for_other(index, part, slot):
         dk, dv = back_part(slot, part)
@@ -340,17 +346,20 @@
         mine = keep[3, part, pl.ds(pl.multiple_of(dp * 16, 16), 16), :]
         for step in range(1, 8):
             mine = mine + y_recv[part, step].astype(f32)
-        dpk_v[part * 16:part * 16 + 16, :] = mine[:, 0:128]
-        dpv_v[part * 16:part * 16 + 16, :] = mine[:, 128:256]
+        dpk_ref[part * 16:part * 16 + 16, :] = mine[:, 0:128]
+        dpv_ref[part * 16:part * 16 + 16, :] = mine[:, 128:256]
 
     def own_keys():
-        dk, dv = back(0, TOKENS, 0, sv_v[...])
-        dsk_v[...] = dk.astype(bf16)
-        dsv_v[...] = dv.astype(bf16)
+        dk, dv = back(0, TOKENS, 0)
+        dsk_ref[...] = dk.astype(bf16)
+        dsv_ref[...] = dv.astype(bf16)
+
+    def attended(head):
+        out_ref[:, head * 128:(head + 1) * 128] = acc[:, head_cols(head)].T.astype(bf16)
 
     def queries_gradient(head):
         turned = dot(kT[...], d_buf[:, head_cols(head)]) * SCALE
-        dq_v[:, head * 128:(head + 1) * 128] = turned.T.astype(bf16)
+        dq_ref[:, head * 128:(head + 1) * 128] = turned.T.astype(bf16)
 
     opposite(0)
     opposite(1)
@@ -377,37 +386,27 @@
     to_chips((2, 1), (2, 2))
     own_keys()
     for head in range(HEADS):
+        attended(head)
         queries_gradient(head)
-    store(dsk_v, dsk_ref)
-    store(dsv_v, dsv_ref)
-    store(dq_v, dq_ref)
     for part in range(PARTS):
         exchange(part)
     for part in range(PARTS):
         finish(part)
-    store(dpk_v, dpk_ref)
-    store(dpv_v, dpv_ref)
     for copy in sends:
         copy.wait_send()
-    for copy in stores:
+
+
+def hand_over(*refs):
+    copies = [pltpu.make_async_copy(refs[i], refs[6 + i], refs[12].at[i]) for i in range(6)]
+    for copy in copies:
+        copy.start()
+    for copy in copies:
         copy.wait()
-
-
-def hand_over(*refs):
-    sources, targets, held, (in_s, out_s) = refs[:6], refs[6:12], refs[12:18], refs[18:]
-    loads = [pltpu.make_async_copy(sources[i], held[i], in_s.at[i]) for i in range(6)]
-    stores = [pltpu.make_async_copy(held[i], targets[i], out_s.at[i]) for i in range(6)]
-    for load in loads:
-        load.start()
-    for load, store in zip(loads, stores):
-        load.wait()
-        store.start()
-    for store in stores:
-        store.wait()
 
 
 def shards(queries, suffix_keys, suffix_values, pre_keys, pre_values, segments, d_out):
     anywhere = pl.BlockSpec(memory_space=pl.ANY)
+    inside = pl.BlockSpec(memory_space=pltpu.VMEM)
     dma = pltpu.SemaphoreType.DMA
     shapes = [
         ((TOKENS, HEADS * HEAD_WIDTH), bf16),
@@ -420,9 +419,9 @@
     out_shape = [jax.ShapeDtypeStruct(shape, dtype) for shape, dtype in shapes]
     results = pl.pallas_call(
         kernel,
-        out_shape=out_shape,
+        out_shape=[pltpu.VMEM(shape, dtype) for shape, dtype in shapes],
         in_specs=[anywhere] * 7,
-        out_specs=[anywhere] * 6,
+        out_specs=[inside] * 6,
         scratch_shapes=[
             pltpu.VMEM((TOKENS, HEADS * HEAD_WIDTH), bf16),
             pltpu.VMEM((TOKENS, HEAD_WIDTH), bf16),
@@ -431,7 +430,6 @@
             pltpu.VMEM((OWN, HEAD_WIDTH), bf16),
             pltpu.VMEM((1, TOKENS), jnp.int32),
             pltpu.VMEM((TOKENS, HEADS * HEAD_WIDTH), bf16),
-        ] + [pltpu.VMEM(shape, dtype) for shape, dtype in shapes] + [
             pltpu.VMEM((8, PARTS, 2, PART, HEAD_WIDTH), bf16),
             pltpu.VMEM((256, ROWS), bf16),
             pltpu.VMEM((128, ROWS), bf16),
@@ -450,6 +448,8 @@
             pltpu.VMEM((2, 768, TOKENS), f32),
             pltpu.VMEM((KEYS, ROWS), bf16),
             pltpu.VMEM((KEYS, ROWS), bf16),
+            pltpu.VMEM((KEYS, HEAD_WIDTH), bf16),
+            pltpu.VMEM((KEYS, ROWS), f32),
             pltpu.VMEM((4, PARTS, PART, 256), f32),
             pltpu.VMEM((4, PARTS, PART, 256), bf16),
             pltpu.VMEM((4, PARTS, PART, 256), bf16),
@@ -457,19 +457,20 @@
             pltpu.VMEM((3, PARTS, PART, 256), bf16),
             pltpu.VMEM((PARTS, 8, 16, 256), bf16),
             pltpu.VMEM((PARTS, 8, 16, 256), bf16),
-            dma((7,)), dma((10,)), dma((21,)), dma((8, PARTS)), dma((4, PARTS)), dma((4, PARTS)),
+            dma((7,)), dma((21,)), dma((8, PARTS)), dma((4, PARTS)), dma((4, PARTS)),
             dma((3, PARTS)), dma((3, PARTS)), dma((PARTS, 8)), dma((PARTS, 8)),
         ],
         compiler_params=pltpu.CompilerParams(
-            collective_id=0, has_side_effects=True, vmem_limit_bytes=60 << 20
+            collective_id=0, has_side_effects=True, vmem_limit_bytes=56 << 20
         ),
     )(queries, suffix_keys, suffix_values, pre_keys, pre_values, segments, d_out)
     return pl.pallas_call(
         hand_over,
         out_shape=out_shape,
-        in_specs=[anywhere] * 6,
+        in_specs=[inside] * 6,
         out_specs=[anywhere] * 6,
-        scratch_shapes=[pltpu.VMEM(shape, dtype) for shape, dtype in shapes] + [dma((6,)), dma((6,))],
+        scratch_shapes=[dma((6,))],
+        compiler_params=pltpu.CompilerParams(vmem_limit_bytes=2 << 20),
     )(*results)
 
 

time: 45.6 us -> 41.5 us (0.910)
  the two profiles are of different devices: /device:TPU:1 before, /device:TPU:2 now
where the time goes in v3:
time: 41.5 us; the launch traced here: 41.4 us
  Pallas kernels  40.6 us (98%)
  between operations  0.8 us (2%)
    pallas_call x1, Pallas kernels, shards(): pl.pallas_call(kernel, out_shape=[pltpu.VMEM(shape, dtype) for shape, dty...  39.7 us
    pallas_call x1, Pallas kernels, shards(): pl.pallas_call(hand_over, out_shape=out_shape, in_specs=[inside] * 6, out...  0.93 us

profile of v3, /device:TPU:2, one launch (start us, length us, event | category | flops | bytes accessed | tf_op | source)
XLA Modules:
  0.0 41.4 jit_solution(9358279454414796018)
XLA Ops:
  0.6 39.7 %shard_map.118 = (bf16[256,640]{1,0:T(8,128)(2,1)S(1)}, bf16[256,640]{1,0:T(8,128)(2,1)S(1)}, bf16[256,128]{1,0:T(8,128)(2,1)S(1)}, bf16[256,128]{1,0:T(8,128)(2...) custom-call(bf16[256,640]{1,0:T(8,128)(2,1)} %q_ref.1, bf16[256,128]{1,0:T(8,128)(2,1)} %sk_ref.1, ...), custom_call_target="tpu_custom_call" | custom-call | tf_op jit(solution)/shard_map/pallas_call | solution.py:420
  40.3 0.9 %shard_map.119 = (bf16[256,640]{1,0:T(8,128)(2,1)}, bf16[256,640]{1,0:T(8,128)(2,1)}, bf16[256,128]{1,0:T(8,128)(2,1)}, bf16[256,128]{1,0:T(8,128)(2,1)}, f32[48,128]{1,0:T(8,128)}, /*index=5*/f32[48,128]{1,0:T(8,128)}) custom-call(bf16[256,640]{1,0:T(8,128)(2,1)S(1)} %get-tuple-element.12.refs_0_, bf16[256,640]{1,0:T(8,128)(2,1)S(1)} %get-tuple-element.13.refs_1_, ...), custom_call_target="tpu_custom_call" | custom-call | tf_op jit(solution)/shard_map/pallas_call | solution.py:467

commit v4 on v3

--- a/solution.py
+++ b/solution.py
@@ -25,8 +25,8 @@
     [(2, 1), (3, 1)],
     [(2, 2), (3, 2), (4, 1), (5, 1)],
     [(2, 0), (3, 0), (6, 0), (4, 2), (5, 2)],
-    [(4, 0), (5, 0), (6, 1), (7, 0)],
-    [(6, 2), (7, 1), (7, 2)],
+    [(4, 0), (5, 0), (6, 1), (7, 0), (7, 1)],
+    [(6, 2), (7, 2)],
 ]
 KEYS = TOKENS + 8 * OWN
 START, CHUNK_OF, CHUNKS = {}, {}, []
@@ -39,6 +39,8 @@
     CHUNKS.append((begin, at - begin))
 STRIP = 256
 LANDING = {0: 0, 1: 2, 2: 1, 3: 3}
+ROW_SENT = (0, 2, 1, 0)
+RING = (1,)
 
 
 def dot(left, right):
@@ -68,10 +70,12 @@
     ahead = ((chip + 1 + 2 * core) % 4) * 2 + core
     behind = ((chip + 3 + 2 * core) % 4) * 2 + core
     opposite_chip = ((chip + 2) % 4) * 2 + core
+    ahead_other = ((chip + 1 + 2 * core) % 4) * 2 + (1 - core)
+    behind_other = ((chip + 3 + 2 * core) % 4) * 2 + (1 - core)
     other = chip * 2 + (1 - core)
 
     barrier = pltpu.get_barrier_semaphore()
-    for peer in (ahead, behind, opposite_chip, other):
+    for peer in (ahead, behind, ahead_other, behind_other, opposite_chip, other):
         pl.semaphore_signal(barrier, inc=1, device_id={"ctx": peer}, device_id_type=MESH)
     for step in range(1, 8):
         pl.semaphore_signal(barrier, inc=1, device_id={"dp": (dp + step) % 8}, device_id_type=MESH)
@@ -125,7 +129,7 @@
             rows = slice(owner * PIECE + part * 16, owner * PIECE + part * 16 + 16)
             kv[0, part, 0, owner * 16:owner * 16 + 16, :] = pk_v[rows, :]
             kv[0, part, 1, owner * 16:owner * 16 + 16, :] = pv_v[rows, :]
-    pl.semaphore_wait(barrier, 11)
+    pl.semaphore_wait(barrier, 13)
     for part in (1, 2, 0):
         if part == 0:
             spread(0, 6, part, opposite_chip)
@@ -163,6 +167,8 @@
                 arrived(3, part)
                 if part > 0:
                     spread(3, 6, part, ahead)
+                if part == 2:
+                    spread(3, 7, part, ahead_other)
                 spread(3, 4, part, other)
             if slot == 2:
                 arrived(2, part)
@@ -171,7 +177,7 @@
                 arrived(6, part)
                 spread(6, 7, part, other)
         for slot, part in ARRIVALS[chunk]:
-            if slot in (1, 4, 5, 7):
+            if slot in (1, 4, 5, 7) or (slot, part) == (6, 2):
                 arrived(slot, part)
             ready(slot, part)
 
@@ -243,10 +249,9 @@
             if turn == 0 and index > 0:
                 gather_values(index - 1)
         weight_gradients(index)
-        if steps[index] in ((4, 1), (5, 1)):
-            part = steps[index][0] - 3
-            arrived(6, part)
-            spread(6, 7, part, other)
+        if steps[index] == (4, 1):
+            arrived(6, 1)
+            spread(6, 7, 1, other)
     gather_values(len(steps) - 1)
 
     for head in range(HEADS):
@@ -298,17 +303,17 @@
 
     def to_chips(*places):
         for index, part in places:
-            landed(sib_recv, sib_r, (0, 2, 1)[index], part)
-            if index == 2:
+            landed(sib_recv, sib_r, ROW_SENT[index], part)
+            if index == 2 and part in RING:
                 landed(x_recv, x_r, 0, part)
         for index, part in places:
-            row = (0, 2, 1)[index]
+            row = ROW_SENT[index]
             value = keep[row, part] + sib_recv[row, part].astype(f32)
-            if index == 2:
+            if index == 2 and part in RING:
                 value = value + x_recv[0, part].astype(f32)
             x_send[index, part] = value.astype(bf16)
         for index, part in places:
-            peer = behind if index == 1 else ahead
+            peer = (ahead, behind, ahead, opposite_chip)[index]
             send(x_send.at[index, part], x_recv.at[index, part], x_s.at[index, part], x_r.at[index, part], {"ctx": peer})
 
     def opposite(part):
@@ -333,6 +338,9 @@
         landed(x_recv, x_r, 2, part)
         mine = keep[3, part] + sib_recv[3, part].astype(f32)
         mine = mine + x_recv[1, part].astype(f32) + x_recv[2, part].astype(f32)
+        if part not in RING:
+            landed(x_recv, x_r, 3, part)
+            mine = mine + x_recv[3, part].astype(f32)
         keep[3, part] = mine
         for owner in range(8):
             y_send[part, owner] = mine[owner * 16:owner * 16 + 16, :].astype(bf16)
@@ -362,38 +370,44 @@
         dq_ref[:, head * 128:(head + 1) * 128] = turned.T.astype(bf16)
 
     opposite(0)
+    to_other((0, 0))
     opposite(1)
-    to_other((0, 0), (0, 1))
     opposite(2)
+    to_other((0, 1), (0, 2))
+    to_chips((3, 0))
     sides_other(0)
-    to_other((0, 2), (1, 0), (2, 0))
-    to_chips((0, 0), (0, 1))
     sides_same(0)
+    to_other((1, 0), (2, 0))
+    to_chips((0, 1), (3, 2))
     sides_other(1)
+    sides_same(1)
     to_other((1, 1), (2, 1))
-    to_chips((0, 2), (1, 0))
-    sides_same(1)
+    to_chips((1, 0), (2, 0))
     sides_other(2)
+    sides_same(2)
     to_other((1, 2), (2, 2))
     to_chips((1, 1))
-    sides_same(2)
     own(0)
-    to_other((3, 0))
-    to_chips((1, 2), (2, 0))
     own(1)
+    to_other((3, 0), (3, 1))
+    to_chips((1, 2), (2, 2))
+    to_chips((2, 1))
     own(2)
-    to_other((3, 1), (3, 2))
-    to_chips((2, 1), (2, 2))
     own_keys()
+    to_other((3, 2))
+    for head in range(2):
+        queries_gradient(head)
+    exchange(0)
+    for head in range(2, HEADS):
+        queries_gradient(head)
     for head in range(HEADS):
         attended(head)
-        queries_gradient(head)
-    for part in range(PARTS):
-        exchange(part)
+    exchange(1)
+    exchange(2)
+    for copy in sends:
+        copy.wait_send()
     for part in range(PARTS):
         finish(part)
-    for copy in sends:
-        copy.wait_send()
 
 
 def hand_over(*refs):
@@ -453,12 +467,12 @@
             pltpu.VMEM((4, PARTS, PART, 256), f32),
             pltpu.VMEM((4, PARTS, PART, 256), bf16),
             pltpu.VMEM((4, PARTS, PART, 256), bf16),
-            pltpu.VMEM((3, PARTS, PART, 256), bf16),
-            pltpu.VMEM((3, PARTS, PART, 256), bf16),
+            pltpu.VMEM((4, PARTS, PART, 256), bf16),
+            pltpu.VMEM((4, PARTS, PART, 256), bf16),
             pltpu.VMEM((PARTS, 8, 16, 256), bf16),
             pltpu.VMEM((PARTS, 8, 16, 256), bf16),
             dma((7,)), dma((21,)), dma((8, PARTS)), dma((4, PARTS)), dma((4, PARTS)),
-            dma((3, PARTS)), dma((3, PARTS)), dma((PARTS, 8)), dma((PARTS, 8)),
+            dma((4, PARTS)), dma((4, PARTS)), dma((PARTS, 8)), dma((PARTS, 8)),
         ],
         compiler_params=pltpu.CompilerParams(
             collective_id=0, has_side_effects=True, vmem_limit_bytes=56 << 20

time: 41.5 us -> 41 us (0.988)
  Pallas kernels: 40.6 us -> 40.1 us
    pallas_call x1, Pallas kernels: 39.7 us -> 39.1 us  [shards(): pl.pallas_call(kernel, out_shape=[pltpu.VMEM(shape, dtype) for shape, dty...]
where the time goes in v4:
time: 41 us; the launch traced here: 40.9 us
  Pallas kernels  40.1 us (98%)
  between operations  0.8 us (2%)
    pallas_call x1, Pallas kernels, shards(): pl.pallas_call(kernel, out_shape=[pltpu.VMEM(shape, dtype) for shape, dty...  39.1 us
    pallas_call x1, Pallas kernels, shards(): pl.pallas_call(hand_over, out_shape=out_shape, in_specs=[inside] * 6, out...  0.93 us

profile of v4, /device:TPU:2, one launch (start us, length us, event | category | flops | bytes accessed | tf_op | source)
XLA Modules:
  0.0 40.9 jit_solution(14699394875614657501)
XLA Ops:
  0.6 39.1 %shard_map.118 = (bf16[256,640]{1,0:T(8,128)(2,1)S(1)}, bf16[256,640]{1,0:T(8,128)(2,1)S(1)}, bf16[256,128]{1,0:T(8,128)(2,1)S(1)}, bf16[256,128]{1,0:T(8,128)(2...) custom-call(bf16[256,640]{1,0:T(8,128)(2,1)} %q_ref.1, bf16[256,128]{1,0:T(8,128)(2,1)} %sk_ref.1, ...), custom_call_target="tpu_custom_call" | custom-call | tf_op jit(solution)/shard_map/pallas_call | solution.py:434
  39.8 0.9 %shard_map.119 = (bf16[256,640]{1,0:T(8,128)(2,1)}, bf16[256,640]{1,0:T(8,128)(2,1)}, bf16[256,128]{1,0:T(8,128)(2,1)}, bf16[256,128]{1,0:T(8,128)(2,1)}, f32[48,128]{1,0:T(8,128)}, /*index=5*/f32[48,128]{1,0:T(8,128)}) custom-call(bf16[256,640]{1,0:T(8,128)(2,1)S(1)} %get-tuple-element.12.refs_0_, bf16[256,640]{1,0:T(8,128)(2,1)S(1)} %get-tuple-element.13.refs_1_, ...), custom_call_target="tpu_custom_call" | custom-call | tf_op jit(solution)/shard_map/pallas_call | solution.py:481

commit v5 on v4

--- a/solution.py
+++ b/solution.py
@@ -40,7 +40,7 @@
 STRIP = 256
 LANDING = {0: 0, 1: 2, 2: 1, 3: 3}
 ROW_SENT = (0, 2, 1, 0)
-RING = (1,)
+RING = ()
 
 
 def dot(left, right):
@@ -378,7 +378,7 @@
     sides_other(0)
     sides_same(0)
     to_other((1, 0), (2, 0))
-    to_chips((0, 1), (3, 2))
+    to_chips((3, 1), (3, 2))
     sides_other(1)
     sides_same(1)
     to_other((1, 1), (2, 1))
@@ -386,12 +386,11 @@
     sides_other(2)
     sides_same(2)
     to_other((1, 2), (2, 2))
-    to_chips((1, 1))
+    to_chips((1, 1), (2, 1))
     own(0)
     own(1)
     to_other((3, 0), (3, 1))
     to_chips((1, 2), (2, 2))
-    to_chips((2, 1))
     own(2)
     own_keys()
     to_other((3, 2))

time: 41 us -> 41.1 us (level)
  no operation moved by 1% of the time
where the time goes in v5:
time: 41.1 us; the launch traced here: 40.9 us
  Pallas kernels  40.1 us (98%)
  between operations  0.8 us (2%)
    pallas_call x1, Pallas kernels, shards(): pl.pallas_call(kernel, out_shape=[pltpu.VMEM(shape, dtype) for shape, dty...  39.2 us
    pallas_call x1, Pallas kernels, shards(): pl.pallas_call(hand_over, out_shape=out_shape, in_specs=[inside] * 6, out...  0.93 us

profile of v5, /device:TPU:2, one launch (start us, length us, event | category | flops | bytes accessed | tf_op | source)
XLA Modules:
  0.0 40.9 jit_solution(12062012070430123491)
XLA Ops:
  0.6 39.2 %shard_map.118 = (bf16[256,640]{1,0:T(8,128)(2,1)S(1)}, bf16[256,640]{1,0:T(8,128)(2,1)S(1)}, bf16[256,128]{1,0:T(8,128)(2,1)S(1)}, bf16[256,128]{1,0:T(8,128)(2...) custom-call(bf16[256,640]{1,0:T(8,128)(2,1)} %q_ref.1, bf16[256,128]{1,0:T(8,128)(2,1)} %sk_ref.1, ...), custom_call_target="tpu_custom_call" | custom-call | tf_op jit(solution)/shard_map/pallas_call | solution.py:433
  39.9 0.9 %shard_map.119 = (bf16[256,640]{1,0:T(8,128)(2,1)}, bf16[256,640]{1,0:T(8,128)(2,1)}, bf16[256,128]{1,0:T(8,128)(2,1)}, bf16[256,128]{1,0:T(8,128)(2,1)}, f32[48,128]{1,0:T(8,128)}, /*index=5*/f32[48,128]{1,0:T(8,128)}) custom-call(bf16[256,640]{1,0:T(8,128)(2,1)S(1)} %get-tuple-element.12.refs_0_, bf16[256,640]{1,0:T(8,128)(2,1)S(1)} %get-tuple-element.13.refs_1_, ...), custom_call_target="tpu_custom_call" | custom-call | tf_op jit(solution)/shard_map/pallas_call | solution.py:480
